TPU v7x, 128 devices: a whole 4x4x4 slice. The times are simulated.
128 devices in a mesh: grid: 64 (over x, y, z_lo, core), col: 2 (over z_hi).
Axes of the slice: x: 4, y: 4, z: 4 (z_hi: 2, z_lo: 2; z = z_hi * 2 + z_lo), core: 2. Of those that a mesh axis runs over, the one named last changes fastest.
Arguments:
- orbitals: bfloat16 [884736, 256], P(('grid', 'col')), may hold values from -6 to 6
- points: int32 [1024], replicated, may hold values from 0 to 884735, as said below
- cinv: bfloat16 [1024, 256], replicated, may hold values from -0.1875 to 0.1875
Outputs:
- potential: bfloat16 [256, 884736], P(None, ('grid', 'col'))
- coupling: float32 [1024, 256], P(('grid', 'col'))
Inputs may be any that keep to these rules, and one draw needn't show every extreme that they name: `points`: 1024 distinct grid rows.
All inputs are finite; a program needn't handle non-finite values.
Results may differ from a plain program's by a relative error of at most 0.0046.
Values may be sent and summed in bfloat16 or wider, within the bound.
A program may use at most 192 MiB of HBM per device.

v0:
```python
import functools
import math

import jax
import jax.numpy as jnp
import ml_dtypes
import numpy as np
from jax import lax
from jax.experimental import pallas as pl
from jax.experimental.pallas import tpu as pltpu
from jax.sharding import PartitionSpec as P

NX = 96
NMU = 1024
RANKS = 128
CHIPS = 64
LINES = 8
TILE = LINES * NX
OWN = 72
PAD = 80
AXES = ("grid", "col")
MESH = pl.DeviceIdType.MESH

screening = 0.25


def rank_id():
    return lax.axis_index("grid") * 2 + lax.axis_index("col")


def device(rank):
    return {"grid": rank // 2, "col": lax.rem(rank, 2)}


def basis(size):
    index = np.arange(size)
    angle = (index[:, None] * index[None, :] % size) * (2.0 * math.pi / size)
    return (np.cos(angle) + np.sin(angle)) / math.sqrt(size)


def two_terms(table):
    high = table.astype(np.float32).astype(ml_dtypes.bfloat16)
    low = (table - high.astype(np.float64)).astype(np.float32).astype(ml_dtypes.bfloat16)
    return high, low


def line_tables():
    table = np.einsum("pc,lm->plmc", basis(NX), np.eye(LINES)).reshape(TILE, TILE)
    return two_terms(table)


def split(values):
    high = values.astype(jnp.bfloat16)
    return high, (values - high.astype(jnp.float32)).astype(jnp.bfloat16)


def dot(a, b):
    return jnp.dot(a, b, preferred_element_type=jnp.float32)


def twice(high):
    return jnp.concatenate([high, high], axis=0)


def parity_of(pair):
    return lax.rem(pair // 8 + pair // 2 + pair, 2)


def owner(p, half):
    pair = p - CHIPS
    first = p // 2 * 4 + lax.rem(p, 2)
    second = pair * 4 + 2 + lax.rem(half + parity_of(jnp.maximum(pair, 0)), 2)
    return jnp.where(p < CHIPS, first, second)


def whole_kernel(
    picked_ref, cinv_ref, basis_ref, terms_ref, orb_hbm, high_hbm, low_hbm,
    pot_ref, part_ref,
    orb, high, low, pair, hat0, hat1, send0, send1, recv0, recv1, field, back0, back1,
    rows, gathered, mine, spread, parts, middle, total, turned,
    sum_sem, all_sem, forth_sem, back_sem, own_sem, load_sem,
):
    hats, sends, recvs, backs = (hat0, hat1), (send0, send1), (recv0, recv1), (back0, back1)
    me = rank_id()
    chip = me // 4 * 2 + lax.rem(me, 2)
    core = lax.rem(me // 2, 2)
    my_p = jnp.where(core == 0, chip, CHIPS + chip // 2)
    my_half = lax.rem(parity_of(chip // 2) + lax.rem(chip, 2), 2)

    loads = [
        pltpu.make_async_copy(source, target, load_sem.at[i])
        for i, (source, target) in enumerate(((orb_hbm, orb), (high_hbm, high), (low_hbm, low)))
    ]
    for load in loads:
        load.start()

    def peer(k):
        return lax.rem(me + k * 37, RANKS)

    barrier = pltpu.get_barrier_semaphore()

    def greet(k, _):
        pl.semaphore_signal(barrier, inc=1, device_id=device(peer(k)), device_id_type=MESH)
        return 0

    lax.fori_loop(1, RANKS, greet, 0)
    pl.semaphore_wait(barrier, RANKS - 1)

    def remote(source, target, sems, rank):
        return pltpu.make_async_remote_copy(
            src_ref=source,
            dst_ref=target,
            send_sem=sems.at[0],
            recv_sem=sems.at[1],
            device_id=device(rank),
            device_id_type=MESH,
        )

    def bytes_of(ref, count, sem):
        block = ref.at[pl.ds(0, count)]
        pltpu.make_async_copy(block, block, sem).wait()

    def exchange(source_of, target, sems, local_sem):
        local = pltpu.make_async_copy(source_of(me), target.at[me], local_sem)
        local.start()

        def go(k, _):
            rank = peer(k)
            remote(source_of(rank), target.at[me], sems, rank).start()
            return 0

        lax.fori_loop(1, RANKS, go, 0)
        local.wait()
        bytes_of(target, RANKS - 1, sems.at[0])
        bytes_of(target, RANKS - 1, sems.at[1])

    exchange(lambda d: picked_ref.at[d], gathered, sum_sem.at[0], own_sem.at[0])
    mine[...] = jnp.sum(gathered[...].astype(jnp.float32), axis=0).astype(jnp.bfloat16)
    exchange(lambda d: mine, spread, all_sem, own_sem.at[1])

    def place(i, _):
        parts_of = [spread[2 * i + j].astype(jnp.float32) for j in range(2)]
        block = [jnp.concatenate([b[:8], b[8:]], axis=1) for b in parts_of]
        rows[pl.ds(pl.multiple_of(16 * i, 16), 16), :] = jnp.concatenate(block, axis=0).astype(jnp.bfloat16)
        return 0

    lax.fori_loop(0, RANKS // 2, place, 0)
    norms = jnp.sum(jnp.square(rows[...].astype(jnp.float32)), axis=1, keepdims=True)
    weights = norms * (jnp.sum(norms) * (1.0 / (NMU * 65536.0)))
    mean = jnp.sum(weights * cinv_ref[...].astype(jnp.float32), axis=0, keepdims=True)

    for load in loads:
        load.wait()

    def fit(step, _):
        here = pl.ds(pl.multiple_of(step * TILE, TILE), TILE)
        product = lax.dot_general(
            orb[here, :], rows[...], (((1,), (1,)), ((), ())), preferred_element_type=jnp.float32
        ) * (1.0 / 16.0)
        squared = (product * product).astype(jnp.bfloat16)
        pair[here, :] = squared
        theta = dot(squared, cinv_ref[...]) - mean
        top, rest = split(theta)
        block = dot(high[...], top) + (dot(low[...], top) + dot(high[...], rest))
        block = block.reshape(NX, LINES, 256)
        lines = pl.ds(pl.multiple_of(step * LINES, LINES), LINES)
        hat0[:, lines, :] = block[:, :, :128]
        hat1[:, lines, :] = block[:, :, 128:]
        return 0

    lax.fori_loop(0, OWN // LINES, fit, 0)

    first_p = me * NX // RANKS

    for half in range(2):
        active = (core == 0) | (my_half == half)
        hat, sent, landed, sems = hats[half], sends[half], recvs[half], forth_sem.at[half]

        def pack(p, _, hat=hat, sent=sent):
            block = jnp.concatenate([hat[p], jnp.zeros((PAD - OWN, 128), jnp.float32)], axis=0)
            sent[p] = block.astype(jnp.bfloat16)
            return 0

        lax.fori_loop(0, NX, pack, 0)

        def go(k, _, sent=sent, landed=landed, sems=sems, half=half):
            p = lax.rem(first_p + k * 37, NX)
            rank = owner(p, half)

            @pl.when(rank != me)
            def _():
                remote(sent.at[p], landed.at[me], sems, rank).start()

            return 0

        lax.fori_loop(0, NX, go, 0)

        @pl.when(active)
        def _(sent=sent, landed=landed, half=half):
            pltpu.make_async_copy(sent.at[my_p], landed.at[me], own_sem.at[2 + half]).start()

    unit = 2.0 * math.pi / NX

    def signed(index):
        return jnp.where(index < NX // 2, index, index - NX).astype(jnp.float32) * unit

    along_a = signed(lax.broadcasted_iota(jnp.int32, (NX, NX), 1))
    along_c = signed(jnp.full((NX, NX), my_p, jnp.int32))
    base = along_a * along_a + along_c * along_c

    def build(kb, _):
        along_b = signed(jnp.full((NX, NX), kb, jnp.int32))
        squared = base + along_b * along_b
        weight = jnp.where(squared > 0, 1.0 / (squared + screening), 0.0)
        top, rest = split(basis_ref[...] * weight)
        table = terms_ref[...]
        full = dot(top, table[:, :NX]) + (dot(top, table[:, NX:]) + dot(rest, table[:, :NX]))
        top, rest = split(full)
        middle[kb] = jnp.concatenate([top, rest], axis=1)
        return 0

    lax.fori_loop(0, NX // 2 + 1, build, 0)

    for half in range(2):
        active = (core == 0) | (my_half == half)
        sent, landed, sems = sends[half], recvs[half], forth_sem.at[half]

        @pl.when(active)
        def _(sent=sent, landed=landed, sems=sems, half=half):
            bytes_of(landed, RANKS - 1, sems.at[1])
            bytes_of(sent, NX - 1, sems.at[0])
            pltpu.make_async_copy(sent.at[my_p], landed.at[me], own_sem.at[2 + half]).wait()
            solve(landed, field, middle, terms_ref)
            pltpu.make_async_copy(landed.at[me], backs[half].at[my_p], own_sem.at[4 + half]).start()

            def go(k, _):
                rank = peer(k)
                remote(landed.at[rank], backs[half].at[my_p], back_sem.at[half], rank).start()
                return 0

            lax.fori_loop(1, RANKS, go, 0)

        @pl.when(jnp.logical_not(active))
        def _(sent=sent, sems=sems):
            bytes_of(sent, NX, sems.at[0])

    for half in range(2):
        active = (core == 0) | (my_half == half)
        back, hat = backs[half], hat0

        @pl.when(active)
        def _(back=back, half=half):
            bytes_of(back, NX - 1, back_sem.at[half, 1])
            pltpu.make_async_copy(recvs[half].at[me], back.at[my_p], own_sem.at[4 + half]).wait()

        @pl.when(jnp.logical_not(active))
        def _(back=back, half=half):
            bytes_of(back, NX, back_sem.at[half, 1])

        def unpack(p, _, back=back, hat=hat):
            hat[p] = back[p].astype(jnp.float32)[:OWN]
            return 0

        lax.fori_loop(0, NX, unpack, 0)

        def finish(i, _, hat=hat, half=half):
            turns = []
            for t in range(3):
                lines = pl.ds(pl.multiple_of((3 * i + t) * LINES, LINES), LINES)
                turns.append(hat[:, lines, :].reshape(TILE, 128).T)
            block = jnp.concatenate(turns, axis=0).astype(jnp.bfloat16)
            pot = (dot(block, high[...]) + dot(block, low[...])).astype(jnp.bfloat16)
            term = None
            for t in range(3):
                here = pl.ds(pl.multiple_of((3 * i + t) * TILE, TILE), TILE)
                part = pot[128 * t : 128 * t + 128]
                pot_ref[pl.ds(128 * half, 128), here] = part
                product = dot(part, pair[here, :])
                term = product if term is None else term + product
            total[...] = jnp.where(i == 0, 0.0, total[...]) + term
            return 0

        lax.fori_loop(0, OWN // LINES // 3, finish, 0)
        turned[half] = total[...].T * (math.sqrt(NMU) / float(NX**3))

        @pl.when(active)
        def _(half=half):
            bytes_of(recvs[half], RANKS - 1, back_sem.at[half, 0])

    def lay(d, _):
        here = pl.ds(pl.multiple_of(8 * d, 8), 8)
        parts[d] = jnp.concatenate([turned[0, here, :], turned[1, here, :]], axis=0).astype(jnp.bfloat16)
        return 0

    lax.fori_loop(0, RANKS, lay, 0)
    exchange(lambda d: parts.at[d], spread, sum_sem.at[1], own_sem.at[6])
    part_ref[...] = jnp.sum(spread[...].astype(jnp.float32), axis=0)


def solve(landed, field, middle, terms_ref):
    def rows_of(u, plane):
        return pl.ds(pl.multiple_of(288 * u + 96 * plane, 96), 96)

    def forward(i, _):
        wholes = [
            jnp.concatenate([landed[8 * i + 4 * j + v].astype(jnp.float32)[:OWN] for v in range(4)], axis=0)
            for j in range(2)
        ]
        for plane in range(3):
            values = jnp.concatenate([w[96 * plane : 96 * plane + 96] for w in wholes], axis=1)
            result = dot(terms_ref[...], twice(values.astype(jnp.bfloat16)))
            for j in range(2):
                field[rows_of(2 * i + j, plane), :] = result[:, 128 * j : 128 * j + 128]
        return 0

    lax.fori_loop(0, 16, forward, 0)

    def across(kb, other):
        table = middle[kb]
        places = [pl.ds(at, NX, stride=NX) for at in (kb, other)]
        top, rest = split(jnp.concatenate([field[place, :] for place in places], axis=1))
        result = dot(table, twice(top)) + dot(table[:, :NX], rest)
        for j in range(2):
            field[places[j], :] = result[:, 128 * j : 128 * j + 128]

    def alone(kb):
        table, place = middle[kb], pl.ds(kb, NX, stride=NX)
        top, rest = split(field[place, :])
        field[place, :] = dot(table, twice(top)) + dot(table[:, :NX], rest)

    def inner(i, _):
        for j in range(2):
            kb = 2 * i + 1 + j
            across(kb, NX - kb)
        return 0

    lax.fori_loop(0, 23, inner, 0)
    across(47, 49)
    alone(0)
    alone(48)

    def backward(i, _):
        planes = []
        for plane in range(3):
            values = jnp.concatenate([field[rows_of(2 * i + j, plane), :] for j in range(2)], axis=1)
            top, rest = split(values)
            planes.append(dot(terms_ref[...], twice(top)) + dot(terms_ref[:, :NX], rest))
        whole = jnp.concatenate(planes, axis=0)
        for j in range(2):
            for v in range(4):
                part = whole[OWN * v : OWN * v + OWN, 128 * j : 128 * j + 128]
                part = jnp.concatenate([part, jnp.zeros((PAD - OWN, 128), jnp.float32)], axis=0)
                landed[8 * i + 4 * j + v] = part.astype(jnp.bfloat16)
        return 0

    lax.fori_loop(0, 16, backward, 0)


def everything(picked, cinv, orbitals):
    table = basis(NX)
    high, low = line_tables()
    terms = np.concatenate(two_terms(table), axis=1)
    vmem = pl.BlockSpec(memory_space=pltpu.VMEM)
    hbm = pl.BlockSpec(memory_space=pl.ANY)
    bf, f32 = jnp.bfloat16, jnp.float32
    local_rows = orbitals.shape[0]
    dma = pltpu.SemaphoreType.DMA
    return pl.pallas_call(
        whole_kernel,
        out_shape=(
            jax.ShapeDtypeStruct((256, local_rows), bf),
            jax.ShapeDtypeStruct((16, 128), f32),
        ),
        in_specs=[vmem] * 4 + [hbm] * 3,
        out_specs=(vmem, vmem),
        scratch_shapes=[
            pltpu.VMEM((local_rows, 256), bf),
            pltpu.VMEM((TILE, TILE), bf),
            pltpu.VMEM((TILE, TILE), bf),
            pltpu.VMEM((local_rows, NMU), bf),
            pltpu.VMEM((NX, OWN, 128), f32),
            pltpu.VMEM((NX, OWN, 128), f32),
            pltpu.VMEM((NX, PAD, 128), bf),
            pltpu.VMEM((NX, PAD, 128), bf),
            pltpu.VMEM((RANKS, PAD, 128), bf),
            pltpu.VMEM((RANKS, PAD, 128), bf),
            pltpu.VMEM((NX * NX, 128), f32),
            pltpu.VMEM((NX, PAD, 128), bf),
            pltpu.VMEM((NX, PAD, 128), bf),
            pltpu.VMEM((NMU, 256), bf),
            pltpu.VMEM((RANKS, 16, 128), bf),
            pltpu.VMEM((16, 128), bf),
            pltpu.VMEM((RANKS, 16, 128), bf),
            pltpu.VMEM((RANKS, 16, 128), bf),
            pltpu.VMEM((NX // 2 + 1, NX, 2 * NX), bf),
            pltpu.VMEM((128, NMU), f32),
            pltpu.VMEM((2, NMU, 128), f32),
            dma((2, 2)),
            dma((2,)),
            dma((2, 2)),
            dma((2, 2)),
            dma((7,)),
            dma((3,)),
        ],
        compiler_params=pltpu.CompilerParams(
            collective_id=0, has_side_effects=True, vmem_limit_bytes=58 * 2**20
        ),
    )(
        picked, cinv, jnp.asarray(table.astype(np.float32)), jnp.asarray(terms),
        orbitals, jnp.asarray(high), jnp.asarray(low),
    )


def local(orbitals, points, cinv):
    local_rows, orbital_count = orbitals.shape
    offset = points - rank_id() * local_rows
    inside = (offset >= 0) & (offset < local_rows)
    picked = jnp.take(orbitals, jnp.clip(offset, 0, local_rows - 1), axis=0)
    picked = jnp.where(inside[:, None], picked, jnp.zeros_like(picked))
    picked = picked.reshape(RANKS, 8, 2, 128).swapaxes(1, 2).reshape(RANKS, 16, 128)
    potential, part = everything(picked, cinv, orbitals)
    return (potential, jnp.concatenate([part[:8], part[8:]], axis=1))


def solution(mesh):
    in_specs = (P(AXES, None), P(), P())
    out_specs = (P(None, AXES), P(AXES, None))
    return jax.shard_map(local, mesh=mesh, in_specs=in_specs, out_specs=out_specs, check_vma=False)
```

profile of v0, /device:TPU:1, one launch (start us, length us, event | category | flops | bytes accessed | tf_op | source)
XLA Modules:
  0.0 220.9 jit_solution(4391400546406414159)
XLA Ops:
  0.6 0.7 compare_and_fusion.1
  1.3 0.7 fusion.2
  2.0 0.1 broadcast_in_dim.28
  2.1 0.1 broadcast_in_dim.30
  2.2 5.9 %gather_fusion = bf16[1024,256]{1,0:T(8,128)(2,1)S(1)} fusion(bf16[6912,256]{1,0:T(8,128)(2,1)} %orb_hbm.1, s32[1024]{0:T(1024)S(1)} %fusion.2), kind=kCustom, calls=%fused_computation | custom fusion | bytes 1052672 | tf_op jit(solution)/shard_map/jit(_take)/gather | solution.py:418
  8.2 1.1 fusion.1.picked_ref
  9.3 206.3 %shard_map.86 = (bf16[256,6912]{1,0:T(8,128)(2,1)}, f32[16,128]{1,0:T(8,128)}) custom-call(bf16[128,16,128]{2,1,0:T(8,128)(2,1)} %fusion.1.picked_ref, bf16[1024,256]{1,0:T(8,128)(2,1)} %cinv_ref.1, f32[96,96]{1,0:T(8,128)} %constant.41.clone.basis_ref, bf16[96,192]{1,0:T(8,128)(2,1)} %constant.42.clone.terms_ref, bf16[6912,256]{1,0:T(8,128)(2,1)} %orb_hbm.1, ...), custom_call_target="tpu_custom_call" | custom-call | tf_op jit(solution)/shard_map/pallas_call | solution.py:368
  215.6 0.7 fusion.3
  216.2 0.6 pad_maximum_fusion
  216.8 4.0 %copy.10 = bf16[256,6912]{1,0:T(8,128)(2,1)} copy(bf16[256,6912]{1,0:T(8,128)(2,1)} %get-tuple-element.12) | data formatting | bytes 7077888
where the time goes:
time: 221 us
  Pallas kernels  206 us (93%)
  local copies, waits for them, and re-layouts  10.8 us (5%)
  other arithmetic  3.13 us (1%)
    pallas_call x1, Pallas kernels, everything(): pl.pallas_call(whole_kernel, out_shape=(jax.ShapeDtypeStruct((256, local_...  206 us
    gather x1, local copies, waits for them, and re-layouts, local(): picked = jnp.take(orbitals, jnp.clip(offset, 0, local_rows - 1), axis=0)  5.92 us

commit v1 on v0

v1 whole, which is shorter than its diff:
```python
import functools
import math

import jax
import jax.numpy as jnp
import ml_dtypes
import numpy as np
from jax import lax
from jax.experimental import pallas as pl
from jax.experimental.pallas import tpu as pltpu
from jax.sharding import PartitionSpec as P

NX = 96
NMU = 1024
RANKS = 128
CHIPS = 64
LINES = 8
TILE = LINES * NX
OWN = 72
MAIN = 64
BLOCK = 144
AXES = ("grid", "col")
MESH = pl.DeviceIdType.MESH

screening = 0.25


def rank_id():
    return lax.axis_index("grid") * 2 + lax.axis_index("col")


def device(rank):
    return {"grid": rank // 2, "col": lax.rem(rank, 2)}


def basis(size):
    index = np.arange(size)
    angle = (index[:, None] * index[None, :] % size) * (2.0 * math.pi / size)
    return (np.cos(angle) + np.sin(angle)) / math.sqrt(size)


def two_terms(table):
    high = table.astype(np.float32).astype(ml_dtypes.bfloat16)
    low = (table - high.astype(np.float64)).astype(np.float32).astype(ml_dtypes.bfloat16)
    return high, low


def line_tables():
    table = np.einsum("pc,lm->plmc", basis(NX), np.eye(LINES)).reshape(TILE, TILE)
    return two_terms(table)


def split(values):
    high = values.astype(jnp.bfloat16)
    return high, (values - high.astype(jnp.float32)).astype(jnp.bfloat16)


def dot(a, b):
    return jnp.dot(a, b, preferred_element_type=jnp.float32)


def twice(high):
    return jnp.concatenate([high, high], axis=0)


def parity_of(pair):
    return lax.rem(pair // 8 + pair // 2 + pair, 2)


def owner(p, half):
    pair = p - CHIPS
    first = p // 2 * 4 + lax.rem(p, 2)
    second = pair * 4 + 2 + lax.rem(half + parity_of(jnp.maximum(pair, 0)), 2)
    return jnp.where(p < CHIPS, first, second)


def whole_kernel(
    offset_ref, cinv_ref, basis_ref, terms_ref, orb_hbm, high_hbm, low_hbm,
    pot_ref, part_ref,
    orb, high, low, pair, sent, landed, field, back, back_tail,
    rows, picked, gathered, mine, spread, parts, middle, total, wide,
    sum_sem, all_sem, forth_sem, back_sem, own_sem, load_sem,
):
    me = rank_id()
    chip = me // 4 * 2 + lax.rem(me, 2)
    core = lax.rem(me // 2, 2)
    my_p = jnp.where(core == 0, chip, CHIPS + chip // 2)
    my_half = lax.rem(parity_of(chip // 2) + lax.rem(chip, 2), 2)
    on_first, on_second = core == 0, core == 1

    loads = [
        pltpu.make_async_copy(source, target, load_sem.at[i])
        for i, (source, target) in enumerate(((orb_hbm, orb), (high_hbm, high), (low_hbm, low)))
    ]
    for load in loads:
        load.start()

    def peer(k):
        return lax.rem(me + k * 37, RANKS)

    barrier = pltpu.get_barrier_semaphore()

    def greet(k, _):
        pl.semaphore_signal(barrier, inc=1, device_id=device(peer(k)), device_id_type=MESH)
        return 0

    lax.fori_loop(1, RANKS, greet, 0)

    def remote(source, target, send_sem, recv_sem, rank):
        return pltpu.make_async_remote_copy(
            src_ref=source,
            dst_ref=target,
            send_sem=send_sem,
            recv_sem=recv_sem,
            device_id=device(rank),
            device_id_type=MESH,
        )

    def bytes_of(ref, count, size, sem):
        block = ref.at[pl.ds(0, count), pl.ds(0, size), :]
        pltpu.make_async_copy(block, block, sem).wait()

    def exchange(source_of, target, sems, local_sem):
        local = pltpu.make_async_copy(source_of(me), target.at[me], local_sem)
        local.start()

        def go(k, _):
            rank = peer(k)
            remote(source_of(rank), target.at[me], sems.at[0], sems.at[1], rank).start()
            return 0

        lax.fori_loop(1, RANKS, go, 0)
        local.wait()
        bytes_of(target, RANKS - 1, 16, sems.at[0])
        bytes_of(target, RANKS - 1, 16, sems.at[1])

    def to_blocks(values):
        halves = [values[:, 128 * h : 128 * h + 128].reshape(RANKS, 8, 128) for h in range(2)]
        return jnp.concatenate(halves, axis=1)

    loads[0].wait()
    wide[...] = jnp.zeros_like(wide)

    def pick(step, _):
        here = pl.ds(pl.multiple_of(step * TILE, TILE), TILE)
        block = orb[here, :]
        for part in range(4):
            some = pl.ds(256 * part, 256)
            index = lax.broadcasted_iota(jnp.int32, (256, TILE), 1)
            match = index == (offset_ref[some, :] - step * TILE)
            wide[some, :] += dot(jnp.where(match, 1.0, 0.0).astype(jnp.bfloat16), block)
        return 0

    lax.fori_loop(0, OWN // LINES, pick, 0)
    picked[...] = to_blocks(wide[...]).astype(jnp.bfloat16)
    pl.semaphore_wait(barrier, RANKS - 1)
    exchange(lambda d: picked.at[d], gathered, sum_sem.at[0], own_sem.at[0])
    mine[...] = jnp.sum(gathered[...].astype(jnp.float32), axis=0).astype(jnp.bfloat16)
    exchange(lambda d: mine, spread, all_sem, own_sem.at[1])
    whole = spread[...].astype(jnp.float32)
    whole = [whole[:, 8 * h : 8 * h + 8].reshape(NMU, 128) for h in range(2)]
    rows[...] = jnp.concatenate(whole, axis=1).astype(jnp.bfloat16)
    norms = jnp.sum(jnp.square(rows[...].astype(jnp.float32)), axis=1, keepdims=True)
    weights = norms * (jnp.sum(norms) * (1.0 / (NMU * 65536.0)))
    mean = jnp.sum(weights * cinv_ref[...].astype(jnp.float32), axis=0, keepdims=True)

    def eight(step):
        here = pl.ds(pl.multiple_of(step * TILE, TILE), TILE)
        product = lax.dot_general(
            orb[here, :], rows[...], (((1,), (1,)), ((), ())), preferred_element_type=jnp.float32
        ) * (1.0 / 16.0)
        squared = (product * product).astype(jnp.bfloat16)
        pair[here, :] = squared
        theta = dot(squared, cinv_ref[...]) - mean
        results = []
        for line in range(LINES):
            top, rest = split(theta[NX * line : NX * line + NX])
            results.append(dot(terms_ref[...], twice(top)) + dot(terms_ref[:, :NX], rest))
        return [
            jnp.swapaxes(jnp.stack([r[:, 128 * h : 128 * h + 128] for r in results], axis=0), 0, 1)
            for h in range(2)
        ]

    def fit(step, _):
        first, second = eight(2 * step), eight(2 * step + 1)
        for h, base in enumerate((0, MAIN + 16)):
            lines = pl.ds(pl.multiple_of(base + 16 * step, 16), 16)
            sent[:, lines, :] = jnp.concatenate([first[h], second[h]], axis=1).astype(jnp.bfloat16)
        return 0

    first_p = me * NX // RANKS

    def forth(half, part):
        def go(k, _):
            p = lax.rem(first_p + k * 37, NX)
            rank = owner(p, half)

            def start(begin, size, sem):
                lines = pl.ds(begin, size)
                sems = forth_sem.at[sem]
                remote(sent.at[p, lines, :], landed.at[me, lines, :], sems.at[0], sems.at[1], rank).start()

            @pl.when(rank != me)
            def _():
                if part == 0:
                    start(0 if half == 0 else 80, 32, half)
                elif half == 0:
                    start(32, 48, 0)
                else:
                    start(112, 32, 1)

                    @pl.when(p >= CHIPS)
                    def _():
                        start(64, 16, 2)

            return 0

        lax.fori_loop(0, NX, go, 0)

    lax.fori_loop(0, 2, fit, 0)
    forth(0, 0)
    forth(1, 0)
    lax.fori_loop(2, 4, fit, 0)
    tail = eight(8)
    sent[:, pl.ds(MAIN, 16), :] = jnp.concatenate(tail, axis=1).astype(jnp.bfloat16)
    forth(0, 1)
    forth(1, 1)
    own_forth = pltpu.make_async_copy(sent.at[my_p], landed.at[me], own_sem.at[2])
    own_forth.start()

    unit = 2.0 * math.pi / NX

    def signed(index):
        return jnp.where(index < NX // 2, index, index - NX).astype(jnp.float32) * unit

    along_a = signed(lax.broadcasted_iota(jnp.int32, (NX, NX), 1))
    along_c = signed(jnp.full((NX, NX), my_p, jnp.int32))
    base = along_a * along_a + along_c * along_c

    def build(kb, _):
        along_b = signed(jnp.full((NX, NX), kb, jnp.int32))
        squared = base + along_b * along_b
        weight = jnp.where(squared > 0, 1.0 / (squared + screening), 0.0)
        top, rest = split(basis_ref[...] * weight)
        table = terms_ref[...]
        full = dot(top, table[:, :NX]) + (dot(top, table[:, NX:]) + dot(rest, table[:, :NX]))
        top, rest = split(full)
        middle[kb] = jnp.concatenate([top, rest], axis=1)
        return 0

    lax.fori_loop(0, NX // 2 + 1, build, 0)
    total[...] = jnp.zeros_like(total)
    loads[1].wait()
    loads[2].wait()
    own_forth.wait()

    def respond(half, rank):
        def start(begin, size, target, sem):
            source = landed.at[rank, pl.ds(begin, size), :]
            sems = back_sem.at[sem]
            remote(source, target, sems.at[0], sems.at[1], rank).start()

        def at(begin, size):
            return back.at[my_p, pl.ds(begin, size), :]

        @pl.when((rank != me) & on_first)
        def _():
            if half == 0:
                start(0, 64, at(0, 64), 0)
            else:
                start(64, 80, at(64, 80), 2)

        @pl.when((rank != me) & on_second)
        def _():
            if half == 0:
                start(0, 80, at(0, 80), 1)
            else:
                start(80, 64, at(80, 64), 3)
                start(64, 16, back_tail.at[chip // 2], 4)

    for half in range(2):
        active = on_first | (my_half == half)

        @pl.when(on_first)
        def _(half=half):
            bytes_of(landed, RANKS - 1, 80 if half == 0 else 64, forth_sem.at[half, 1])

        @pl.when(on_second & (my_half == half))
        def _(half=half):
            bytes_of(landed, RANKS - 1, 80 if half == 0 else 64, forth_sem.at[half, 1])
            if half == 1:
                bytes_of(landed, RANKS - 1, 16, forth_sem.at[2, 1])

        @pl.when(active)
        def _(half=half):
            solve(half, landed, field, middle, terms_ref, functools.partial(respond, half), me // 8)

    def keep(test, pieces):
        @pl.when(test)
        def _():
            for i, (begin, size, target) in enumerate(pieces):
                source = landed.at[me, pl.ds(begin, size), :]
                copy = pltpu.make_async_copy(source, target, own_sem.at[3 + i])
                copy.start()
                copy.wait()

    mine_back = lambda begin, size: (begin, size, back.at[my_p, pl.ds(begin, size), :])
    keep(on_first, [mine_back(0, BLOCK)])
    keep(on_second & (my_half == 0), [mine_back(0, 80)])
    keep(on_second & (my_half == 1), [mine_back(80, 64), (64, 16, back_tail.at[chip // 2])])

    def left(test, count, size, sem):
        @pl.when(test)
        def _():
            bytes_of(sent, count, size, forth_sem.at[sem, 0])

    owns = [on_first | (my_half == half) for half in range(2)]
    for half, size in ((0, 80), (1, 64)):
        left(owns[half], NX - 1, size, half)
        left(jnp.logical_not(owns[half]), NX, size, half)
    last = on_second & (my_half == 1)
    left(last, 31, 16, 2)
    left(jnp.logical_not(last), 32, 16, 2)

    def arrived(test, count, size, sem, ref):
        @pl.when(test)
        def _():
            bytes_of(ref, count, size, back_sem.at[sem, 1])

    def potentials(blocks, half, first):
        turns = [block.reshape(TILE, 128).T for block in blocks]
        block = jnp.concatenate(turns, axis=0).astype(jnp.bfloat16)
        pot = (dot(block, high[...]) + dot(block, low[...])).astype(jnp.bfloat16)
        term = None
        for t in range(len(blocks)):
            here = pl.ds(pl.multiple_of((first + t) * TILE, TILE), TILE)
            some = pot[128 * t : 128 * t + 128]
            pot_ref[pl.ds(128 * half, 128), here] = some
            product = dot(some, pair[here, :])
            term = product if term is None else term + product
        total[pl.ds(128 * half, 128), :] += term

    for half in range(2):
        second = on_second & (my_half == half)
        if half == 0:
            counts = ((0, 64, on_first, 64, back), (1, 32, second, 80, back))
        else:
            counts = ((2, 64, on_first, 80, back), (3, 32, second, 64, back), (4, 32, second, 16, back_tail))
        for sem, count, mine_too, size, ref in counts:
            arrived(mine_too, count - 1, size, sem, ref)
            arrived(jnp.logical_not(mine_too), count, size, sem, ref)

        def finish(s, _, half=half):
            lines = pl.ds(pl.multiple_of((80 if half else 0) + 16 * s, 16), 16)
            block = back[:, lines, :].astype(jnp.float32)
            potentials([block[:, :8], block[:, 8:]], half, 2 * s)
            return 0

        lax.fori_loop(0, 4, finish, 0)

    block = back[:, pl.ds(MAIN, 16), :].astype(jnp.float32)
    other = back_tail[...].astype(jnp.float32)
    potentials([block[:, :8]], 0, 8)
    potentials([jnp.concatenate([block[:CHIPS, 8:], other[:, 8:]], axis=0)], 1, 8)

    factor = math.sqrt(NMU) / float(NX**3)
    parts[...] = to_blocks(total[...].T * factor).astype(jnp.bfloat16)
    exchange(lambda d: parts.at[d], spread, sum_sem.at[1], own_sem.at[5])
    part_ref[...] = jnp.sum(spread[...].astype(jnp.float32), axis=0)

    def gone(test, size, sem):
        @pl.when(test)
        def _():
            bytes_of(landed, RANKS - 1, size, back_sem.at[sem, 0])

    gone(on_first, 64, 0)
    gone(on_first, 80, 2)
    gone(on_second & (my_half == 0), 80, 1)
    gone(on_second & (my_half == 1), 64, 3)
    gone(on_second & (my_half == 1), 16, 4)


def solve(half, landed, field, middle, terms_ref, respond, first):
    base = 80 if half else 0
    main, rest_of = pl.ds(base, MAIN), pl.ds(MAIN, 16)

    def block_of(rank):
        upper = landed[rank, main, :].astype(jnp.float32)
        lower = landed[rank, rest_of, :].astype(jnp.float32)[8 * half : 8 * half + 8]
        return jnp.concatenate([upper, lower], axis=0)

    def forward(i, _):
        for pack in range(2):
            start = 2 * i + pack
            wholes = [
                jnp.concatenate([block_of(8 * start + 4 * j + v) for v in range(4)], axis=0) for j in range(2)
            ]
            for plane in range(3):
                values = jnp.concatenate([w[96 * plane : 96 * plane + 96] for w in wholes], axis=1)
                result = dot(terms_ref[...], twice(values.astype(jnp.bfloat16)))
                for j in range(2):
                    field[3 * (2 * start + j) + plane] = result[:, 128 * j : 128 * j + 128]
        return 0

    lax.fori_loop(0, 8, forward, 0)

    def inner(i, _):
        place = pl.ds(pl.multiple_of(8 * i, 8), 8)
        values = jnp.swapaxes(field[:, place, :], 0, 1)
        results = []
        for j in range(8):
            kb = 8 * i + j
            table = middle[jnp.minimum(kb, NX - kb)]
            top, rest = split(values[j])
            results.append(dot(table, twice(top)) + dot(table[:, :NX], rest))
        field[:, place, :] = jnp.swapaxes(jnp.stack(results, axis=0), 0, 1)
        return 0

    lax.fori_loop(0, NX // 8, inner, 0)

    def backward(i, _):
        start = lax.rem(i + first, 16)
        planes = []
        for plane in range(3):
            values = jnp.concatenate([field[3 * (2 * start + j) + plane] for j in range(2)], axis=1)
            top, rest = split(values)
            planes.append(dot(terms_ref[...], twice(top)) + dot(terms_ref[:, :NX], rest))
        whole = jnp.concatenate(planes, axis=0)
        for j in range(2):
            for v in range(4):
                rank = 8 * start + 4 * j + v
                part = whole[OWN * v : OWN * v + OWN, 128 * j : 128 * j + 128]
                landed[rank, main, :] = part[:MAIN].astype(jnp.bfloat16)
                lower = landed[rank, rest_of, :].astype(jnp.float32)
                pieces = [part[MAIN:], lower[8:]] if half == 0 else [lower[:8], part[MAIN:]]
                landed[rank, rest_of, :] = jnp.concatenate(pieces, axis=0).astype(jnp.bfloat16)
        for v in range(8):
            respond(8 * start + v)
        return 0

    lax.fori_loop(0, 16, backward, 0)


def everything(offset, cinv, orbitals):
    table = basis(NX)
    high, low = line_tables()
    terms = np.concatenate(two_terms(table), axis=1)
    vmem = pl.BlockSpec(memory_space=pltpu.VMEM)
    hbm = pl.BlockSpec(memory_space=pl.ANY)
    bf, f32 = jnp.bfloat16, jnp.float32
    local_rows = orbitals.shape[0]
    dma = pltpu.SemaphoreType.DMA
    return pl.pallas_call(
        whole_kernel,
        out_shape=(
            jax.ShapeDtypeStruct((256, local_rows), bf),
            jax.ShapeDtypeStruct((16, 128), f32),
        ),
        in_specs=[vmem] * 4 + [hbm] * 3,
        out_specs=(vmem, vmem),
        scratch_shapes=[
            pltpu.VMEM((local_rows, 256), bf),
            pltpu.VMEM((TILE, TILE), bf),
            pltpu.VMEM((TILE, TILE), bf),
            pltpu.VMEM((local_rows, NMU), bf),
            pltpu.VMEM((NX, BLOCK, 128), bf),
            pltpu.VMEM((RANKS, BLOCK, 128), bf),
            pltpu.VMEM((NX, NX, 128), f32),
            pltpu.VMEM((NX, BLOCK, 128), bf),
            pltpu.VMEM((NX - CHIPS, 16, 128), bf),
            pltpu.VMEM((NMU, 256), bf),
            pltpu.VMEM((RANKS, 16, 128), bf),
            pltpu.VMEM((RANKS, 16, 128), bf),
            pltpu.VMEM((16, 128), bf),
            pltpu.VMEM((RANKS, 16, 128), bf),
            pltpu.VMEM((RANKS, 16, 128), bf),
            pltpu.VMEM((NX // 2 + 1, NX, 2 * NX), bf),
            pltpu.VMEM((256, NMU), f32),
            pltpu.VMEM((NMU, 256), f32),
            dma((2, 2)),
            dma((2,)),
            dma((3, 2)),
            dma((5, 2)),
            dma((6,)),
            dma((3,)),
        ],
        compiler_params=pltpu.CompilerParams(
            collective_id=0, has_side_effects=True, vmem_limit_bytes=58 * 2**20
        ),
    )(
        offset, cinv, jnp.asarray(table.astype(np.float32)), jnp.asarray(terms),
        orbitals, jnp.asarray(high), jnp.asarray(low),
    )


def local(orbitals, points, cinv):
    offset = points - rank_id() * orbitals.shape[0]
    potential, part = everything(offset.reshape(NMU, 1), cinv, orbitals)
    return (potential, jnp.concatenate([part[:8], part[8:]], axis=1))


def solution(mesh):
    in_specs = (P(AXES, None), P(), P())
    out_specs = (P(None, AXES), P(AXES, None))
    return jax.shard_map(local, mesh=mesh, in_specs=in_specs, out_specs=out_specs, check_vma=False)
```

time: 221 us -> 179 us (0.81)
  Pallas kernels: 206 us -> 171 us
  local copies, waits for them, and re-layouts: 10.8 us -> 5.73 us
    pallas_call x1, Pallas kernels: 206 us -> 171 us  [everything(): pl.pallas_call(whole_kernel, out_shape=(jax.ShapeDtypeStruct((256, local_...]
    gather x1 -> x0, local copies, waits for them, and re-layouts: 5.92 us -> none  [local(): picked = jnp.take(orbitals, jnp.clip(offset, 0, local_rows - 1), axis=0)]
where the time goes in v1:
time: 179 us
  Pallas kernels  171 us (96%)
  local copies, waits for them, and re-layouts  5.73 us (3%)
    pallas_call x1, Pallas kernels, everything(): pl.pallas_call(whole_kernel, out_shape=(jax.ShapeDtypeStruct((256, local_...  171 us
    unnamed x1, local copies, waits for them, and re-layouts  4.02 us

profile of v1, /device:TPU:1, one launch (start us, length us, event | category | flops | bytes accessed | tf_op | source)
XLA Modules:
  0.0 178.8 jit_solution(6177469269453757919)
XLA Ops:
  0.6 0.7 broadcast_subtract_fusion
  1.3 1.0 copy.9.offset_ref
  2.4 171.1 %shard_map.86 = (bf16[256,6912]{1,0:T(8,128)(2,1)}, f32[16,128]{1,0:T(8,128)}) custom-call(s32[1024,1]{1,0:T(8,128)} %copy.9.offset_ref, bf16[1024,256]{1,0:T(8,128)(2,1)} %cinv_ref.1, f32[96,96]{1,0:T(8,128)} %constant.20.clone.basis_ref, bf16[96,192]{1,0:T(8,128)(2,1)} %constant.21.clone.terms_ref, bf16[6912,256]{1,0:T(8,128)(2,1)} %orb_hbm.1, ...), custom_call_target="tpu_custom_call" | custom-call | tf_op jit(solution)/shard_map/pallas_call | solution.py:453
  173.5 0.7 fusion
  174.2 0.6 pad_maximum_fusion
  174.8 4.0 %copy.11 = bf16[256,6912]{1,0:T(8,128)(2,1)} copy(bf16[256,6912]{1,0:T(8,128)(2,1)} %get-tuple-element.10) | data formatting | bytes 7077888

commit v2 on v1

--- a/solution.py
+++ b/solution.py
@@ -75,9 +75,9 @@
 
 
 def whole_kernel(
-    offset_ref, cinv_ref, basis_ref, terms_ref, orb_hbm, high_hbm, low_hbm,
-    pot_ref, part_ref,
-    orb, high, low, pair, sent, landed, field, back, back_tail,
+    points_ref, cinv_ref, basis_ref, terms_ref, orb_hbm, high_hbm, low_hbm,
+    pot_hbm, part_ref,
+    pot_ref, orb, high, low, pair, sent, landed, field, back, back_tail,
     rows, picked, gathered, mine, spread, parts, middle, total, wide,
     sum_sem, all_sem, forth_sem, back_sem, own_sem, load_sem,
 ):
@@ -147,7 +147,7 @@
         for part in range(4):
             some = pl.ds(256 * part, 256)
             index = lax.broadcasted_iota(jnp.int32, (256, TILE), 1)
-            match = index == (offset_ref[some, :] - step * TILE)
+            match = index == (points_ref[some, :] - (me * orb.shape[0] + step * TILE))
             wide[some, :] += dot(jnp.where(match, 1.0, 0.0).astype(jnp.bfloat16), block)
         return 0
 
@@ -190,7 +190,7 @@
 
     first_p = me * NX // RANKS
 
-    def forth(half, part):
+    def forth(half, begin, size):
         def go(k, _):
             p = lax.rem(first_p + k * 37, NX)
             rank = owner(p, half)
@@ -200,31 +200,26 @@
                 sems = forth_sem.at[sem]
                 remote(sent.at[p, lines, :], landed.at[me, lines, :], sems.at[0], sems.at[1], rank).start()
 
-            @pl.when(rank != me)
-            def _():
-                if part == 0:
-                    start(0 if half == 0 else 80, 32, half)
-                elif half == 0:
-                    start(32, 48, 0)
-                else:
-                    start(112, 32, 1)
-
-                    @pl.when(p >= CHIPS)
-                    def _():
-                        start(64, 16, 2)
-
+            if half == 0:
+                pl.when(rank != me)(lambda: start(begin, size, 0))
+            else:
+                pl.when((rank != me) & (p < CHIPS))(lambda: start(80, 64, 1))
+                pl.when((rank != me) & (p >= CHIPS))(lambda: start(64, 80, 2))
             return 0
 
         lax.fori_loop(0, NX, go, 0)
 
-    lax.fori_loop(0, 2, fit, 0)
-    forth(0, 0)
-    forth(1, 0)
-    lax.fori_loop(2, 4, fit, 0)
+    def fit_and_send(step, _):
+        fit(step, 0)
+        pl.when(step == 0)(lambda: forth(0, 0, 16))
+        pl.when(step == 2)(lambda: forth(0, 16, 32))
+        return 0
+
+    lax.fori_loop(0, 4, fit_and_send, 0)
     tail = eight(8)
     sent[:, pl.ds(MAIN, 16), :] = jnp.concatenate(tail, axis=1).astype(jnp.bfloat16)
-    forth(0, 1)
-    forth(1, 1)
+    forth(0, 48, 32)
+    forth(1, None, None)
     own_forth = pltpu.make_async_copy(sent.at[my_p], landed.at[me], own_sem.at[2])
     own_forth.start()
 
@@ -263,14 +258,14 @@
         def at(begin, size):
             return back.at[my_p, pl.ds(begin, size), :]
 
-        @pl.when((rank != me) & on_first)
+        @pl.when(on_first)
         def _():
             if half == 0:
                 start(0, 64, at(0, 64), 0)
             else:
                 start(64, 80, at(64, 80), 2)
 
-        @pl.when((rank != me) & on_second)
+        @pl.when(on_second)
         def _():
             if half == 0:
                 start(0, 80, at(0, 80), 1)
@@ -287,13 +282,17 @@
 
         @pl.when(on_second & (my_half == half))
         def _(half=half):
-            bytes_of(landed, RANKS - 1, 80 if half == 0 else 64, forth_sem.at[half, 1])
-            if half == 1:
-                bytes_of(landed, RANKS - 1, 16, forth_sem.at[2, 1])
+            bytes_of(landed, RANKS - 1, 80, forth_sem.at[2 * half, 1])
 
         @pl.when(active)
         def _(half=half):
-            solve(half, landed, field, middle, terms_ref, functools.partial(respond, half), me // 8)
+            solve(half, landed, field, middle, terms_ref)
+
+            def answer(k, _):
+                respond(half, peer(k))
+                return 0
+
+            lax.fori_loop(1, RANKS, answer, 0)
 
     def keep(test, pieces):
         @pl.when(test)
@@ -314,13 +313,14 @@
         def _():
             bytes_of(sent, count, size, forth_sem.at[sem, 0])
 
-    owns = [on_first | (my_half == half) for half in range(2)]
-    for half, size in ((0, 80), (1, 64)):
-        left(owns[half], NX - 1, size, half)
-        left(jnp.logical_not(owns[half]), NX, size, half)
+    owns = on_first | (my_half == 0)
+    left(owns, NX - 1, 80, 0)
+    left(jnp.logical_not(owns), NX, 80, 0)
+    left(on_first, CHIPS - 1, 64, 1)
+    left(on_second, CHIPS, 64, 1)
     last = on_second & (my_half == 1)
-    left(last, 31, 16, 2)
-    left(jnp.logical_not(last), 32, 16, 2)
+    left(last, NX - CHIPS - 1, 80, 2)
+    left(jnp.logical_not(last), NX - CHIPS, 80, 2)
 
     def arrived(test, count, size, sem, ref):
         @pl.when(test)
@@ -363,10 +363,15 @@
     potentials([block[:, :8]], 0, 8)
     potentials([jnp.concatenate([block[:CHIPS, 8:], other[:, 8:]], axis=0)], 1, 8)
 
+    store = pltpu.make_async_copy(pot_ref, pot_hbm, load_sem.at[3])
+    store.start()
+
     factor = math.sqrt(NMU) / float(NX**3)
     parts[...] = to_blocks(total[...].T * factor).astype(jnp.bfloat16)
     exchange(lambda d: parts.at[d], spread, sum_sem.at[1], own_sem.at[5])
-    part_ref[...] = jnp.sum(spread[...].astype(jnp.float32), axis=0)
+    share = jnp.sum(spread[...].astype(jnp.float32), axis=0)
+    part_ref[...] = jnp.concatenate([share[:8], share[8:]], axis=1)
+    store.wait()
 
     def gone(test, size, sem):
         @pl.when(test)
@@ -380,7 +385,7 @@
     gone(on_second & (my_half == 1), 16, 4)
 
 
-def solve(half, landed, field, middle, terms_ref, respond, first):
+def solve(half, landed, field, middle, terms_ref):
     base = 80 if half else 0
     main, rest_of = pl.ds(base, MAIN), pl.ds(MAIN, 16)
 
@@ -419,7 +424,7 @@
     lax.fori_loop(0, NX // 8, inner, 0)
 
     def backward(i, _):
-        start = lax.rem(i + first, 16)
+        start = i
         planes = []
         for plane in range(3):
             values = jnp.concatenate([field[3 * (2 * start + j) + plane] for j in range(2)], axis=1)
@@ -434,14 +439,12 @@
                 lower = landed[rank, rest_of, :].astype(jnp.float32)
                 pieces = [part[MAIN:], lower[8:]] if half == 0 else [lower[:8], part[MAIN:]]
                 landed[rank, rest_of, :] = jnp.concatenate(pieces, axis=0).astype(jnp.bfloat16)
-        for v in range(8):
-            respond(8 * start + v)
         return 0
 
     lax.fori_loop(0, 16, backward, 0)
 
 
-def everything(offset, cinv, orbitals):
+def everything(points, cinv, orbitals):
     table = basis(NX)
     high, low = line_tables()
     terms = np.concatenate(two_terms(table), axis=1)
@@ -454,11 +457,12 @@
         whole_kernel,
         out_shape=(
             jax.ShapeDtypeStruct((256, local_rows), bf),
-            jax.ShapeDtypeStruct((16, 128), f32),
+            jax.ShapeDtypeStruct((8, 256), f32),
         ),
         in_specs=[vmem] * 4 + [hbm] * 3,
-        out_specs=(vmem, vmem),
+        out_specs=(hbm, vmem),
         scratch_shapes=[
+            pltpu.VMEM((256, local_rows), bf),
             pltpu.VMEM((local_rows, 256), bf),
             pltpu.VMEM((TILE, TILE), bf),
             pltpu.VMEM((TILE, TILE), bf),
@@ -482,21 +486,19 @@
             dma((3, 2)),
             dma((5, 2)),
             dma((6,)),
-            dma((3,)),
+            dma((4,)),
         ],
         compiler_params=pltpu.CompilerParams(
             collective_id=0, has_side_effects=True, vmem_limit_bytes=58 * 2**20
         ),
     )(
-        offset, cinv, jnp.asarray(table.astype(np.float32)), jnp.asarray(terms),
+        points, cinv, jnp.asarray(table.astype(np.float32)), jnp.asarray(terms),
         orbitals, jnp.asarray(high), jnp.asarray(low),
     )
 
 
 def local(orbitals, points, cinv):
-    offset = points - rank_id() * orbitals.shape[0]
-    potential, part = everything(offset.reshape(NMU, 1), cinv, orbitals)
-    return (potential, jnp.concatenate([part[:8], part[8:]], axis=1))
+    return everything(points.reshape(NMU, 1), cinv, orbitals)
 
 
 def solution(mesh):

time: 179 us -> 168 us (0.939)
  Pallas kernels: 171 us -> 160 us
    pallas_call x1, Pallas kernels: 171 us -> 160 us  [everything(): pl.pallas_call(whole_kernel, out_shape=(jax.ShapeDtypeStruct((256, local_...]
    unnamed x1 -> x4, local copies, waits for them, and re-layouts: 4.02 us -> 4.63 us
where the time goes in v2:
time: 168 us; the launch traced here: 167 us
  Pallas kernels  160 us (95%)
  local copies, waits for them, and re-layouts  6.34 us (4%)
    pallas_call x1, Pallas kernels, everything(): pl.pallas_call(whole_kernel, out_shape=(jax.ShapeDtypeStruct((256, local_...  160 us
    unnamed x4, local copies, waits for them, and re-layouts  4.63 us

profile of v2, /device:TPU:1, one launch (start us, length us, event | category | flops | bytes accessed | tf_op | source)
XLA Modules:
  0.0 167.1 jit_solution(16720514939385362581)
XLA Ops:
  0.6 1.7 %copy.9.points_ref = s32[1024,1]{1,0:T(8,128)} copy(s32[1024,1]{0,1:T(1,128)} %bitcast.1) | data formatting | bytes 8192 | tf_op jit(solution)/shard_map/reshape | solution.py:501
  2.3 160.1 %shard_map.86 = (bf16[256,6912]{1,0:T(8,128)(2,1)}, f32[8,256]{1,0:T(8,128)}) custom-call(s32[1024,1]{1,0:T(8,128)} %copy.9.points_ref, bf16[1024,256]{1,0:T(8,128)(2,1)} %cinv_ref.1, f32[96,96]{1,0:T(8,128)} %constant.8.clone.basis_ref, bf16[96,192]{1,0:T(8,128)(2,1)} %constant.9.clone.terms_ref, bf16[6912,256]{1,0:T(8,128)(2,1)} %orb_hbm.1, ...), custom_call_target="tpu_custom_call" | custom-call | tf_op jit(solution)/shard_map/pallas_call | solution.py:456
  162.5 0.0 copy-start
  162.5 4.0 %copy.12 = bf16[256,6912]{1,0:T(8,128)(2,1)} copy(bf16[256,6912]{1,0:T(8,128)(2,1)} %get-tuple-element.4) | data formatting | bytes 7077888
  166.5 0.0 copy-done
  166.5 0.6 copy.13
Async XLA Ops:
  162.5 4.0 %copy-start = (f32[8,256]{1,0:T(8,128)S(1)}, f32[8,256]{1,0:T(8,128)}, u32[]{:S(2)}) copy-start(f32[8,256]{1,0:T(8,128)} %get-tuple-element.5) | copy-start | bytes 24580

commit v3 on v2

--- a/solution.py
+++ b/solution.py
@@ -96,7 +96,7 @@
         load.start()
 
     def peer(k):
-        return lax.rem(me + k * 37, RANKS)
+        return lax.rem(me + k * 53, RANKS)
 
     barrier = pltpu.get_barrier_semaphore()
 
@@ -192,7 +192,7 @@
 
     def forth(half, begin, size):
         def go(k, _):
-            p = lax.rem(first_p + k * 37, NX)
+            p = lax.rem(first_p + k * 53, NX)
             rank = owner(p, half)
 
             def start(begin, size, sem):
@@ -249,7 +249,7 @@
     loads[2].wait()
     own_forth.wait()
 
-    def respond(half, rank):
+    def respond(half, late, rank):
         def start(begin, size, target, sem):
             source = landed.at[rank, pl.ds(begin, size), :]
             sems = back_sem.at[sem]
@@ -257,20 +257,24 @@
 
         def at(begin, size):
             return back.at[my_p, pl.ds(begin, size), :]
+
+        if late:
+            start(112, 32, at(112, 32), 5)
+            return
 
         @pl.when(on_first)
         def _():
             if half == 0:
                 start(0, 64, at(0, 64), 0)
             else:
-                start(64, 80, at(64, 80), 2)
+                start(64, 48, at(64, 48), 2)
 
         @pl.when(on_second)
         def _():
             if half == 0:
                 start(0, 80, at(0, 80), 1)
             else:
-                start(80, 64, at(80, 64), 3)
+                start(80, 32, at(80, 32), 3)
                 start(64, 16, back_tail.at[chip // 2], 4)
 
     for half in range(2):
@@ -288,11 +292,13 @@
         def _(half=half):
             solve(half, landed, field, middle, terms_ref)
 
-            def answer(k, _):
-                respond(half, peer(k))
-                return 0
-
-            lax.fori_loop(1, RANKS, answer, 0)
+            for late in range(1 + half):
+
+                def answer(k, _, late=late):
+                    respond(half, late, peer(k))
+                    return 0
+
+                lax.fori_loop(1, RANKS, answer, 0)
 
     def keep(test, pieces):
         @pl.when(test)
@@ -342,26 +348,31 @@
 
     for half in range(2):
         second = on_second & (my_half == half)
-        if half == 0:
-            counts = ((0, 64, on_first, 64, back), (1, 32, second, 80, back))
-        else:
-            counts = ((2, 64, on_first, 80, back), (3, 32, second, 64, back), (4, 32, second, 16, back_tail))
-        for sem, count, mine_too, size, ref in counts:
-            arrived(mine_too, count - 1, size, sem, ref)
-            arrived(jnp.logical_not(mine_too), count, size, sem, ref)
-
         def finish(s, _, half=half):
             lines = pl.ds(pl.multiple_of((80 if half else 0) + 16 * s, 16), 16)
             block = back[:, lines, :].astype(jnp.float32)
             potentials([block[:, :8], block[:, 8:]], half, 2 * s)
             return 0
 
-        lax.fori_loop(0, 4, finish, 0)
-
-    block = back[:, pl.ds(MAIN, 16), :].astype(jnp.float32)
-    other = back_tail[...].astype(jnp.float32)
-    potentials([block[:, :8]], 0, 8)
-    potentials([jnp.concatenate([block[:CHIPS, 8:], other[:, 8:]], axis=0)], 1, 8)
+        if half == 0:
+            counts = ((0, 64, on_first, 64, back), (1, 32, second, 80, back))
+        else:
+            counts = ((2, 64, on_first, 48, back), (3, 32, second, 32, back), (4, 32, second, 16, back_tail))
+        for sem, count, mine_too, size, ref in counts:
+            arrived(mine_too, count - 1, size, sem, ref)
+            arrived(jnp.logical_not(mine_too), count, size, sem, ref)
+        if half == 0:
+            lax.fori_loop(0, 4, finish, 0)
+        else:
+            lax.fori_loop(0, 2, finish, 0)
+            block = back[:, pl.ds(MAIN, 16), :].astype(jnp.float32)
+            other = back_tail[...].astype(jnp.float32)
+            potentials([block[:, :8]], 0, 8)
+            potentials([jnp.concatenate([block[:CHIPS, 8:], other[:, 8:]], axis=0)], 1, 8)
+            late = on_first | second
+            arrived(late, NX - 1, 32, 5, back)
+            arrived(jnp.logical_not(late), NX, 32, 5, back)
+            lax.fori_loop(2, 4, finish, 0)
 
     store = pltpu.make_async_copy(pot_ref, pot_hbm, load_sem.at[3])
     store.start()
@@ -379,10 +390,11 @@
             bytes_of(landed, RANKS - 1, size, back_sem.at[sem, 0])
 
     gone(on_first, 64, 0)
-    gone(on_first, 80, 2)
+    gone(on_first, 48, 2)
     gone(on_second & (my_half == 0), 80, 1)
-    gone(on_second & (my_half == 1), 64, 3)
+    gone(on_second & (my_half == 1), 32, 3)
     gone(on_second & (my_half == 1), 16, 4)
+    gone(on_first | (my_half == 1), 32, 5)
 
 
 def solve(half, landed, field, middle, terms_ref):
@@ -484,7 +496,7 @@
             dma((2, 2)),
             dma((2,)),
             dma((3, 2)),
-            dma((5, 2)),
+            dma((6, 2)),
             dma((6,)),
             dma((4,)),
         ],

time: 168 us -> 163 us (0.970)
  Pallas kernels: 160 us -> 156 us
    pallas_call x1, Pallas kernels: 160 us -> 156 us  [everything(): pl.pallas_call(whole_kernel, out_shape=(jax.ShapeDtypeStruct((256, local_...]
where the time goes in v3:
time: 163 us
  Pallas kernels  156 us (96%)
  local copies, waits for them, and re-layouts  6.34 us (4%)
    pallas_call x1, Pallas kernels, everything(): pl.pallas_call(whole_kernel, out_shape=(jax.ShapeDtypeStruct((256, local_...  156 us
    unnamed x4, local copies, waits for them, and re-layouts  4.63 us

profile of v3, /device:TPU:1, one launch (start us, length us, event | category | flops | bytes accessed | tf_op | source)
XLA Modules:
  0.0 162.6 jit_solution(15166975642065151883)
XLA Ops:
  0.6 1.7 %copy.9.points_ref = s32[1024,1]{1,0:T(8,128)} copy(s32[1024,1]{0,1:T(1,128)} %bitcast.1) | data formatting | bytes 8192 | tf_op jit(solution)/shard_map/reshape | solution.py:513
  2.3 155.6 %shard_map.86 = (bf16[256,6912]{1,0:T(8,128)(2,1)}, f32[8,256]{1,0:T(8,128)}) custom-call(s32[1024,1]{1,0:T(8,128)} %copy.9.points_ref, bf16[1024,256]{1,0:T(8,128)(2,1)} %cinv_ref.1, f32[96,96]{1,0:T(8,128)} %constant.8.clone.basis_ref, bf16[96,192]{1,0:T(8,128)(2,1)} %constant.9.clone.terms_ref, bf16[6912,256]{1,0:T(8,128)(2,1)} %orb_hbm.1, ...), custom_call_target="tpu_custom_call" | custom-call | tf_op jit(solution)/shard_map/pallas_call | solution.py:468
  158.0 0.0 copy-start
  158.0 4.0 %copy.12 = bf16[256,6912]{1,0:T(8,128)(2,1)} copy(bf16[256,6912]{1,0:T(8,128)(2,1)} %get-tuple-element.4) | data formatting | bytes 7077888
  162.0 0.0 copy-done
  162.0 0.6 copy.13
Async XLA Ops:
  158.0 4.0 %copy-start = (f32[8,256]{1,0:T(8,128)S(1)}, f32[8,256]{1,0:T(8,128)}, u32[]{:S(2)}) copy-start(f32[8,256]{1,0:T(8,128)} %get-tuple-element.5) | copy-start | bytes 24580

commit v4 on v3

--- a/solution.py
+++ b/solution.py
@@ -104,7 +104,7 @@
         pl.semaphore_signal(barrier, inc=1, device_id=device(peer(k)), device_id_type=MESH)
         return 0
 
-    lax.fori_loop(1, RANKS, greet, 0)
+    lax.fori_loop(1, RANKS, greet, 0, unroll=4)
 
     def remote(source, target, send_sem, recv_sem, rank):
         return pltpu.make_async_remote_copy(
@@ -129,7 +129,7 @@
             remote(source_of(rank), target.at[me], sems.at[0], sems.at[1], rank).start()
             return 0
 
-        lax.fori_loop(1, RANKS, go, 0)
+        lax.fori_loop(1, RANKS, go, 0, unroll=4)
         local.wait()
         bytes_of(target, RANKS - 1, 16, sems.at[0])
         bytes_of(target, RANKS - 1, 16, sems.at[1])
@@ -207,7 +207,7 @@
                 pl.when((rank != me) & (p >= CHIPS))(lambda: start(64, 80, 2))
             return 0
 
-        lax.fori_loop(0, NX, go, 0)
+        lax.fori_loop(0, NX, go, 0, unroll=4)
 
     def fit_and_send(step, _):
         fit(step, 0)
@@ -298,7 +298,7 @@
                     respond(half, late, peer(k))
                     return 0
 
-                lax.fori_loop(1, RANKS, answer, 0)
+                lax.fori_loop(1, RANKS, answer, 0, unroll=4)
 
     def keep(test, pieces):
         @pl.when(test)

time: 163 us -> 163 us (level)
  no operation moved by 1% of the time
where the time goes in v4:
time: 163 us; the launch traced here: 162 us
  Pallas kernels  155 us (95%)
  local copies, waits for them, and re-layouts  6.34 us (4%)
    pallas_call x1, Pallas kernels, everything(): pl.pallas_call(whole_kernel, out_shape=(jax.ShapeDtypeStruct((256, local_...  155 us
    unnamed x4, local copies, waits for them, and re-layouts  4.63 us

profile of v4, /device:TPU:1, one launch (start us, length us, event | category | flops | bytes accessed | tf_op | source)
XLA Modules:
  0.0 162.4 jit_solution(11383157013668603738)
XLA Ops:
  0.6 1.7 %copy.9.points_ref = s32[1024,1]{1,0:T(8,128)} copy(s32[1024,1]{0,1:T(1,128)} %bitcast.1) | data formatting | bytes 8192 | tf_op jit(solution)/shard_map/reshape | solution.py:513
  2.3 155.5 %shard_map.86 = (bf16[256,6912]{1,0:T(8,128)(2,1)}, f32[8,256]{1,0:T(8,128)}) custom-call(s32[1024,1]{1,0:T(8,128)} %copy.9.points_ref, bf16[1024,256]{1,0:T(8,128)(2,1)} %cinv_ref.1, f32[96,96]{1,0:T(8,128)} %constant.8.clone.basis_ref, bf16[96,192]{1,0:T(8,128)(2,1)} %constant.9.clone.terms_ref, bf16[6912,256]{1,0:T(8,128)(2,1)} %orb_hbm.1, ...), custom_call_target="tpu_custom_call" | custom-call | tf_op jit(solution)/shard_map/pallas_call | solution.py:468
  157.8 0.0 copy-start
  157.8 4.0 %copy.12 = bf16[256,6912]{1,0:T(8,128)(2,1)} copy(bf16[256,6912]{1,0:T(8,128)(2,1)} %get-tuple-element.4) | data formatting | bytes 7077888
  161.8 0.0 copy-done
  161.9 0.6 copy.13
Async XLA Ops:
  157.8 4.0 %copy-start = (f32[8,256]{1,0:T(8,128)S(1)}, f32[8,256]{1,0:T(8,128)}, u32[]{:S(2)}) copy-start(f32[8,256]{1,0:T(8,128)} %get-tuple-element.5) | copy-start | bytes 24580
